TPU v7x, 32 devices: a whole 2x2x4 slice. The times are simulated.
32 devices in a mesh: groups: 2 (over y), ctx: 8 (over z, x), tp: 2 (over core).
Axes of the slice: x: 2, y: 2, z: 4, core: 2. Of those that a mesh axis runs over, the one named last changes fastest.
Arguments:
- hidden: bfloat16 [4096, 8192], P(('groups', 'ctx'), 'tp'), parts along dimension 0, may hold values from -6 to 6
- queries: bfloat16 [4096, 4096], P(('groups', 'ctx'), 'tp'), parts along dimension 0, may hold values from -300 to 300
- weight_buckets: bfloat16 [16, 512, 4, 2, 128], P('ctx', None, 'tp'), may hold values from -0.0625 to 0.0625
- bucket_rows: int32 [16], replicated, may hold values from 0 to 15, each once
- selected: int32 [8, 3], P('groups'), parts along dimension 0, may hold values from 0 to 3, as said below
- counts: int32 [8], P('groups'), parts along dimension 0, may hold values from 1 to 3, as said below
Outputs:
- attended: bfloat16 [4096, 4096], P(('groups', 'ctx'), 'tp'), parts along dimension 0
There are 2 independent parts, one for each index of `groups`. A program takes and returns all parts, laid end to end along the dimension named above; an argument that names none is the same for every part. Nothing has to cross between parts.
Inputs may be any that keep to these rules, and one draw needn't show every extreme that they name: `selected`: row q begins with q; its next counts[q] - 1 entries are distinct blocks before q; entries past counts[q] are block numbers that are not used. counts[q] is at most min(q + 1, 3); the last query block uses all 3. `bucket_rows`: each row block is stored in exactly one bucket.
All inputs are finite; a program needn't handle non-finite values.
Results may differ from a plain program's by a relative error of at most 0.0028.
The roundings to bfloat16 on the way count: a program that leaves them out, or rounds other values in their place, can miss the bound.
Values may be sent and summed in bfloat16 or wider, within the bound.
A program may use at most 128 MiB of HBM per device.

v0:
```python
import math

import jax
import jax.numpy as jnp
from jax import lax
from jax.sharding import PartitionSpec as P

HD = 128
KB = 512
TOPK = 3


masked_score = -1e30


def shards(hidden, queries, weight_buckets, bucket_rows, selected, counts):
    tok_rows = hidden.shape[0]
    ctx_size = lax.axis_size("ctx")
    ctx_index = lax.axis_index("ctx")
    gathered = lax.all_gather(hidden, "tp", axis=1, tiled=True)
    feat_width = gathered.shape[1]
    bucket_count = bucket_rows.shape[0]
    bucket_depth = feat_width // bucket_count
    kv_local = weight_buckets.shape[2]
    kv_width = kv_local * 2 * HD
    arranged = gathered.reshape(tok_rows, bucket_count, bucket_depth)[:, bucket_rows, :]
    arranged = arranged.reshape(tok_rows, feat_width)
    piece = lax.all_gather(weight_buckets, "ctx", axis=0, tiled=True)
    count_rows = piece.shape[0] * bucket_depth
    projected = jnp.dot(
        arranged, piece.reshape(count_rows, kv_width), preferred_element_type=jnp.float32
    )
    key_values = projected.astype(jnp.bfloat16)
    block_count = selected.shape[0]
    block_rows = tok_rows // block_count
    by_block = key_values.reshape(block_count, block_rows, kv_width)
    query_blocks = max(1, tok_rows // KB)
    query_len = min(KB, tok_rows)
    targets = (jnp.arange(ctx_size, dtype=jnp.int32) * tok_rows // KB)[:, None] + jnp.arange(
        query_blocks, dtype=jnp.int32
    )[None, :]
    wanted = selected[targets].reshape(ctx_size, query_blocks * TOPK)
    live = jnp.arange(TOPK, dtype=jnp.int32)[None, None, :] < counts[targets][:, :, None]
    block_tags = jnp.where(live.reshape(ctx_size, query_blocks * TOPK), wanted, -1)
    local_tags = jnp.broadcast_to(
        jnp.arange(query_blocks, dtype=jnp.int32)[:, None], (query_blocks, TOPK)
    )
    local_tags = jnp.broadcast_to(local_tags, block_tags.shape)
    markers = jnp.stack([block_tags, local_tags], axis=-1).astype(jnp.bfloat16)
    outgoing = by_block[wanted]
    heads_local = queries.shape[1] // HD
    group_size = heads_local // kv_local
    score_scale = 1.0 / math.sqrt(HD)
    offsets = jnp.arange(KB, dtype=jnp.int32)
    within = offsets % block_rows * ctx_size + offsets // block_rows
    query_offsets = jnp.arange(query_len, dtype=jnp.int32)

    def one_item(payload, marker):
        block_id = marker[0].astype(jnp.int32)
        is_live = block_id >= 0
        key_block = jnp.maximum(block_id, 0)
        which_block = marker[1].astype(jnp.int32)
        stacked = payload.reshape(KB, kv_local, 2, HD)
        key_pos = key_block * KB + within
        rows_here = queries
        rows_here = rows_here.reshape(query_len, kv_local, group_size, HD)
        query_pos = ctx_index * tok_rows + which_block * query_len + query_offsets
        scores = (
            jnp.einsum(
                "qkgd,skd->kgqs", rows_here, stacked[:, :, 0], preferred_element_type=jnp.float32
            )
            * score_scale
        )
        visible = (key_pos[None, :] <= query_pos[:, None]) & is_live
        scores = jnp.where(visible, scores, masked_score)
        peak = scores.max(axis=-1)
        raised = jnp.exp(scores - peak[..., None])
        total = raised.sum(axis=-1)
        blended = jnp.einsum(
            "kgqs,skd->kgqd",
            raised.astype(jnp.bfloat16),
            stacked[:, :, 1],
            preferred_element_type=jnp.float32,
        )
        return (peak, total, blended)

    payloads = lax.all_to_all(outgoing, "ctx", split_axis=0, concat_axis=0, tiled=True)
    markings = lax.all_to_all(markers, "ctx", split_axis=0, concat_axis=0, tiled=True)

    def handle(position):
        payload = lax.dynamic_index_in_dim(payloads, position, 1, keepdims=False)
        marker = lax.dynamic_index_in_dim(markings[0], position, 0, keepdims=False)
        return one_item(payload, marker)

    peaks, totals, blends = lax.map(handle, jnp.arange(payloads.shape[1], dtype=jnp.int32))
    peaks = peaks.reshape(query_blocks, TOPK, kv_local, group_size, query_len)
    totals = totals.reshape(query_blocks, TOPK, kv_local, group_size, query_len)
    blends = blends.reshape(query_blocks, TOPK, kv_local, group_size, query_len, HD)
    highest = peaks.max(axis=1, keepdims=True)
    factors = jnp.exp(peaks - highest)
    weighted = jnp.sum(factors[..., None] * blends, axis=1)
    normalizer = jnp.sum(factors * totals, axis=1)
    result = weighted / normalizer[..., None]
    return result.transpose(0, 3, 1, 2, 4).reshape(tok_rows, heads_local * HD).astype(jnp.bfloat16)


def solution(mesh):
    placed = (
        P(("groups", "ctx"), "tp"),
        P(("groups", "ctx"), "tp"),
        P("ctx", None, "tp", None, None),
        P(),
        P("groups", None),
        P("groups"),
    )
    return jax.shard_map(
        shards, mesh=mesh, in_specs=placed, out_specs=P(("groups", "ctx"), "tp"), check_vma=False
    )
```

profile of v0, /device:TPU:24, one launch (start us, length us, event | category | flops | bytes accessed | tf_op | source)
XLA Modules:
  0.0 290.7 jit_solution(10133040892088231521)
XLA Ops:
  6.5 0.0 all-gather.3.cloned.1.call-start
  6.6 4.2 %copy.49 = bf16[256,4096]{0,1:T(8,128)(2,1)} copy(bf16[256,4096]{1,0:T(8,128)(2,1)} %param.8) | data formatting | bytes 4194304 | tf_op args[0]
  10.7 0.0 all-gather.3.cloned.1.call-update
  10.8 0.0 all-gather.5.cloned.1.call-start
  10.8 1.1 copy.52
  11.9 0.0 all-gather.5.cloned.1.call-update
  12.0 0.6 gather_fusion.1
  12.6 0.1 copy.47
  12.6 0.6 gather_fusion
  13.3 0.1 copy.65
  13.4 0.6 stack.4.clone
  14.0 6.0 %all-to-all-start = ((bf16[8,3,2]{1,2,0:T(2,128)(2,1)}), bf16[8,3,2]{1,2,0:T(2,128)(2,1)S(1)}, u32[]{:S(2)}, u32[]{:S(2)}) async-start(bf16[8,3,2]{1,2,0:T(2,128)(2,1)} %stack.4.clone), calls=%async_computation | async-start | bytes 8192 | tf_op jit(solution)/shard_map/all_to_all | solution.py:88
  20.0 0.1 copy.54
  20.1 0.1 reshape.253
  20.2 5.6 %all-gather.3.cloned.1.call-done = bf16[256,8192]{0,1:T(8,128)(2,1)} async-done(((bf16[256,4096]{0,1:T(8,128)(2,1)}), bf16[256,8192]{0,1:T(8,128)(2,1)}) %all-gather.3.cloned.1.call-update) | async-done | bytes 4194320 | tf_op jit(solution)/shard_map/all_gather | solution.py:20
  25.8 6.4 %copy.50 = bf16[256,16,512]{2,0,1:T(8,128)(2,1)} copy(bf16[256,16,512]{0,2,1:T(8,128)(2,1)} %bitcast.112) | data formatting | bytes 8388608 | tf_op jit(solution)/shard_map/reshape | solution.py:26
  32.2 5.0 %gather_fusion.2 = bf16[16,256,512]{2,1,0:T(8,128)(2,1)} fusion(bf16[256,16,512]{2,0,1:T(8,128)(2,1)} %copy.50, s32[1024]{0:T(1024)S(1)} %pad_clamp_fusion.1), kind=kCustom, calls=%fused_computation.2 | custom fusion | bytes 8388672 | tf_op jit(solution)/shard_map/gather | solution.py:26
  37.2 6.5 %copy.51 = bf16[256,16,512]{0,2,1:T(8,128)(2,1)} copy(bf16[256,16,512]{2,0,1:T(8,128)(2,1)} %bitcast.109) | data formatting | bytes 8388608 | tf_op jit(solution)/shard_map/gather | solution.py:26
  43.6 108.2 %all-gather.5.cloned.1.call-done = bf16[16,512,2,2,128]{4,1,3,2,0:T(8,128)(2,1)} async-done(((bf16[2,512,2,2,128]{4,1,3,2,0:T(8,128)(2,1)}), bf16[16,512,2,2,128]{4,1,3,2,0:T(8,128)(2,1)}) %all-gather.5.cloned.1.call-update) | async-done | bytes 8388624 | tf_op jit(solution)/shard_map/all_gather | solution.py:28
  151.9 14.6 %copy.53 = bf16[16,512,2,2,128]{1,0,4,3,2:T(8,128)(2,1)} copy(bf16[16,512,2,2,128]{4,1,3,2,0:T(8,128)(2,1)} %all-gather.5.cloned.1.call-done) | data formatting | bytes 16777216 | tf_op jit(solution)/shard_map/all_gather | solution.py:28
  166.5 16.4 %copy.67 = bf16[64,8,16,512]{3,1,2,0:T(8,128)(2,1)} copy(bf16[64,8,16,512]{3,2,1,0:T(8,128)(2,1)} %bitcast.107) | data formatting | bytes 16777216
  182.9 7.3 %convolution_convert_fusion = bf16[256,512]{1,0:T(8,128)(2,1)S(1)} fusion(bf16[256,8192]{0,1:T(8,128)(2,1)} %bitcast.113, bf16[8192,512]{0,1:T(8,128)(2,1)} %bitcast.111), kind=kOutput, calls=%fused_computation.43 | convolution fusion | flops 2147614720 | bytes 12845056 | tf_op jit(solution)/shard_map/dot_general | solution.py:30
  190.2 0.0 copy-start.3
  190.2 1.9 gather_fusion.3
  192.2 0.0 all-to-all-done
  192.2 6.6 %all-to-all-start.1 = ((bf16[8,3,64,512]{3,2,1,0:T(8,128)(2,1)}), bf16[8,3,64,512]{3,2,1,0:T(8,128)(2,1)}, u32[]{:S(2)}, u32[]{:S(2)}) async-start(bf16[8,3,64,512]{3,2,1,0:T(8,128)(2,1)} %bitcast.6), calls=%async_computation.1 | async-start | bytes 3145728 | tf_op jit(solution)/shard_map/all_to_all | solution.py:87
  198.8 0.1 copy.55
  198.9 34.9 %all-to-all-done.1 = bf16[8,3,64,512]{3,2,1,0:T(8,128)(2,1)} async-done(((bf16[8,3,64,512]{3,2,1,0:T(8,128)(2,1)}), bf16[8,3,64,512]{3,2,1,0:T(8,128)(2,1)}, u32[]{:S(2)}, u32[]{:S(2)}) %all-to-all-start.1) | async-done | bytes 1572896 | tf_op jit(solution)/shard_map/all_to_all | solution.py:87
  233.8 42.8 %while.15 = (s32[]{:T(128)}, f32[3,2,8,256]{3,2,1,0:T(8,128)S(1)}, f32[3,2,8,256]{3,2,1,0:T(8,128)S(1)}, f32[3,2,8,256,128]{4,3,2,1,0:T(8,128)}, bf16[8,3,2]{0,2...) while((s32[]{:T(128)}, f32[3,2,8,256]{3,2,1,0:T(8,128)S(1)}, ...), condition=%wide.region_3.4_spmd.clone, body=%wide.region_0.3_spmd.clone.sunk | while | flops 1097072384 | bytes 34741028 | solution.py:95
  233.8 0.7 dynamic_slice.22
  236.5 0.6 fusion.41
  238.5 0.2 compare_and_fusion.2
  238.6 1.1 dynamic-slice_bitcast_fusion.2
  239.7 0.1 reshape.269
  239.9 0.7 fusion.43
  240.6 0.2 copy.85
  240.9 1.6 fusion.44
  242.4 3.8 %bitcast_dynamic-update-slice_fusion.6 = f32[3,2,8,256,128]{4,3,2,1,0:T(8,128)} fusion(f32[3,2,8,256,128]{4,3,2,1,0:T(8,128)} %get-tuple-element.252, s32[]{:T(128)} %get-tuple-element.249, f32[2,512,256,8]{2,1,3,0:T(8,128)S(1)} %get-tuple-element.229, f32[2,8,256]{2,1,0:T(8,128)S(1)} %get-tuple-element.230, ...), kind=kOutput, calls=%fused_computation.13.clone.1 | convolution fusion | flops 545259520 | bytes 10895872 | tf_op jit(solution)/shard_map/while/body/eval_jaxpr/kgqs,skd->kgqd/dot_general | solution.py:79
  246.3 1.7 fusion.45
  248.0 0.7 dynamic_slice.22
  250.8 0.6 fusion.41
  252.8 0.2 compare_and_fusion.2
  252.9 1.1 dynamic-slice_bitcast_fusion.2
  254.0 0.1 reshape.269
  254.2 0.7 fusion.43
  254.9 0.2 copy.85
  255.1 1.6 fusion.44
  256.7 3.8 %bitcast_dynamic-update-slice_fusion.6 = f32[3,2,8,256,128]{4,3,2,1,0:T(8,128)} fusion(f32[3,2,8,256,128]{4,3,2,1,0:T(8,128)} %get-tuple-element.252, s32[]{:T(128)} %get-tuple-element.249, f32[2,512,256,8]{2,1,3,0:T(8,128)S(1)} %get-tuple-element.229, f32[2,8,256]{2,1,0:T(8,128)S(1)} %get-tuple-element.230, ...), kind=kOutput, calls=%fused_computation.13.clone.1 | convolution fusion | flops 545259520 | bytes 10895872 | tf_op jit(solution)/shard_map/while/body/eval_jaxpr/kgqs,skd->kgqd/dot_general | solution.py:79
  260.5 1.7 fusion.45
  262.3 0.7 dynamic_slice.22
  265.0 0.6 fusion.41
  267.0 0.2 compare_and_fusion.2
  267.2 1.1 dynamic-slice_bitcast_fusion.2
  268.3 0.1 reshape.269
  268.4 0.7 fusion.43
  269.1 0.2 copy.85
  269.4 1.6 fusion.44
  270.9 3.8 %bitcast_dynamic-update-slice_fusion.6 = f32[3,2,8,256,128]{4,3,2,1,0:T(8,128)} fusion(f32[3,2,8,256,128]{4,3,2,1,0:T(8,128)} %get-tuple-element.252, s32[]{:T(128)} %get-tuple-element.249, f32[2,512,256,8]{2,1,3,0:T(8,128)S(1)} %get-tuple-element.229, f32[2,8,256]{2,1,0:T(8,128)S(1)} %get-tuple-element.230, ...), kind=kOutput, calls=%fused_computation.13.clone.1 | convolution fusion | flops 545259520 | bytes 10895872 | tf_op jit(solution)/shard_map/while/body/eval_jaxpr/kgqs,skd->kgqd/dot_general | solution.py:79
  274.8 1.7 fusion.45
  276.6 0.0 copy-start.1
  276.6 4.6 %multiply_reduce_fusion = f32[2,8,256,128]{3,2,1,0:T(8,128)S(1)} fusion(f32[3,2,8,256,128]{4,3,2,1,0:T(8,128)} %get-tuple-element.65, f32[3,2,8,256]{3,2,1,0:T(8,128)S(1)} %get-tuple-element.152), kind=kLoop, calls=%fused_computation.40 | loop fusion | flops 2621440 | bytes 8437760 | tf_op jit(solution)/shard_map/reduce_sum | solution.py:101
  281.2 0.7 fusion.27
  281.9 0.5 copy.57
  282.4 1.4 copy.58
  (34 shorter events, 0.2 us)
Async XLA Ops:
  6.5 5.5 %copy-start = (s32[4,3]{1,0:T(4,128)S(1)}, s32[4,3]{1,0:T(4,128)}, u32[]{:S(2)}) copy-start(s32[4,3]{1,0:T(4,128)} %param.12) | copy-start | bytes 148
  6.5 4.3 %copy-start.4 = (bf16[2,512,2,2,128]{4,3,2,1,0:T(2,128)(2,1)S(1)}, bf16[2,512,2,2,128]{4,3,2,1,0:T(2,128)(2,1)}, u32[]{:S(2)}) copy-start(bf16[2,512,2,2,128]{4,3,2,1,0:T(2,128)(2,1)} %param.10) | copy-start | bytes 3145732
  6.5 6.1 %copy-start.2 = (s32[4]{0:T(128)S(1)}, s32[4]{0:T(128)}, u32[]{:S(2)}) copy-start(s32[4]{0:T(128)} %param.13) | copy-start | bytes 52
  6.5 13.7 %copy-start.5 = (s32[16]{0:T(128)S(1)}, s32[16]{0:T(128)}, u32[]{:S(2)}) copy-start(s32[16]{0:T(128)} %param.11) | copy-start | bytes 196
  6.5 19.3 %all-gather.3.cloned.1.call-start = ((), (), s32[]{:S(2)}) async-start(), calls=%async_computation.2 | async-start | bytes 6291456 | tf_op jit(solution)/shard_map/all_gather | solution.py:20
  10.8 141.1 %all-gather.5.cloned.1.call-start = ((), (), s32[]{:S(2)}) async-start(), calls=%async_computation.3 | async-start | bytes 9437184 | tf_op jit(solution)/shard_map/all_gather | solution.py:28
  14.0 178.2 %all-to-all-start = ((bf16[8,3,2]{1,2,0:T(2,128)(2,1)}), bf16[8,3,2]{1,2,0:T(2,128)(2,1)S(1)}, u32[]{:S(2)}, u32[]{:S(2)}) async-start(bf16[8,3,2]{1,2,0:T(2,128)(2,1)} %stack.4.clone), calls=%async_computation | async-start | bytes 8192 | tf_op jit(solution)/shard_map/all_to_all | solution.py:88
  190.2 43.6 %copy-start.3 = (bf16[256,2048]{1,0:T(8,128)(2,1)S(1)}, bf16[256,2048]{1,0:T(8,128)(2,1)}, u32[]{:S(2)}) copy-start(bf16[256,2048]{1,0:T(8,128)(2,1)} %param.9) | copy-start | bytes 3145732
  192.2 41.6 %all-to-all-start.1 = ((bf16[8,3,64,512]{3,2,1,0:T(8,128)(2,1)}), bf16[8,3,64,512]{3,2,1,0:T(8,128)(2,1)}, u32[]{:S(2)}, u32[]{:S(2)}) async-start(bf16[8,3,64,512]{3,2,1,0:T(8,128)(2,1)} %bitcast.6), calls=%async_computation.1 | async-start | bytes 3145728 | tf_op jit(solution)/shard_map/all_to_all | solution.py:87
  276.6 7.3 %copy-start.1 = (s32[4,3]{1,0:T(4,128)S(1)}, s32[4,3]{1,0:T(4,128)}, u32[]{:S(2)}) copy-start(s32[4,3]{1,0:T(4,128)} %param.12) | copy-start | bytes 148
Sparse Core Ops, SparseCore 0:
  10.9 14.8 all-gather.2
  27.9 123.8 all-gather.4
where the time goes:
time: 295 us; the launch traced here: 291 us
  waiting for transfers between devices  149 us (51%)
  local copies, waits for them, and re-layouts  70.7 us (24%)
  matrix products  23.5 us (8%)
  between operations  13.5 us (5%)
  starting transfers between devices  12.7 us (4%)
  other arithmetic  11.1 us (4%)
  loops' own time  10.5 us (4%)
    all_gather x1, waiting for transfers between devices, shards(): piece = lax.all_gather(weight_buckets, 'ctx', axis=0, tiled=True)  108 us
    all_to_all x1, waiting for transfers between devices, shards(): lax.all_to_all(outgoing, 'ctx', split_axis=0, concat_axis=0, tiled=True)  34.9 us
    unnamed x17, local copies, waits for them, and re-layouts  21.9 us
    all_gather x1, local copies, waits for them, and re-layouts, shards(): piece = lax.all_gather(weight_buckets, 'ctx', axis=0, tiled=True)  14.6 us
    dot_general x3, matrix products, one_item(): jnp.einsum('kgqs,skd->kgqd', raised.astype(jnp.bfloat16), stacked[:, :, 1...  11.5 us
    gather x2, local copies, waits for them, and re-layouts, shards(): gathered.reshape(tok_rows, bucket_count, bucket_depth)[:, bucket_rows, :]  11.4 us
    another operation x1, loops' own time, shards(): lax.map(handle, jnp.arange(payloads.shape[1], dtype=jnp.int32))  10.5 us
    dot_general x1, matrix products, shards(): jnp.dot(arranged, piece.reshape(count_rows, kv_width), preferred_element_...  7.29 us
  transfers between devices with their start and end apart: 4, of which 3 were waited for; matrix products, arithmetic and copies ran while one was open for 21% of the time, Pallas kernels for 0%

commit v1 on v0

--- a/solution.py
+++ b/solution.py
@@ -1,8 +1,11 @@
+import functools
 import math
 
 import jax
 import jax.numpy as jnp
 from jax import lax
+from jax.experimental import pallas as pl
+from jax.experimental.pallas import tpu as pltpu
 from jax.sharding import PartitionSpec as P
 
 HD = 128
@@ -13,7 +16,7 @@
 masked_score = -1e30
 
 
-def shards(hidden, queries, weight_buckets, bucket_rows, selected, counts):
+def general_shards(hidden, queries, weight_buckets, bucket_rows, selected, counts):
     tok_rows = hidden.shape[0]
     ctx_size = lax.axis_size("ctx")
     ctx_index = lax.axis_index("ctx")
@@ -104,6 +107,279 @@
     return result.transpose(0, 3, 1, 2, 4).reshape(tok_rows, heads_local * HD).astype(jnp.bfloat16)
 
 
+SUB = 16
+MESH = pl.DeviceIdType.MESH
+MIB = 1 << 20
+
+
+def ring_to_ctx(pos, n):
+    upper = pos // (n // 2)
+    return 2 * pos + upper * (2 * n - 1 - 4 * pos)
+
+
+def ctx_to_ring(ctx, n):
+    return ctx // 2 + (ctx % 2) * (n - 1 - 2 * (ctx // 2))
+
+
+def job_table(rows):
+    units = rows // SUB
+    first = (units + 5) // 6
+    second = (units - 4 * first) // 2
+    sizes = [first, second, first, first, second, first]
+    starts = [sum(sizes[:i]) for i in range(6)]
+    jobs = []
+    for i in range(4):
+        jobs.append((sizes[i] * SUB, starts[i] * SUB, starts[5 - i] * SUB))
+    return jobs
+
+
+def project_kernel(
+    n, kv_rows_piece, rows_ref, hidden_ref, w_ref, kv_ref,
+    feats, wbuf, acc, hid_sem, w_send, w_recv, y_send, y_recv, kv_send, kv_recv,
+):
+    ctx = lax.axis_index("ctx")
+    group = lax.axis_index("groups")
+    core = lax.axis_index("tp")
+    pos = ctx_to_ring(ctx, n)
+    nxt = ring_to_ctx((pos + 1) % n, n)
+    prv = ring_to_ctx((pos + n - 1) % n, n)
+    other_core = {"tp": 1 - core}
+    other_group = {"groups": 1 - group}
+    depth = feats.shape[2]
+    in_half = feats.shape[0] // 2
+    per_owner = rows_ref.shape[0] // n
+
+    barrier = pltpu.get_barrier_semaphore()
+    for peer in ({"ctx": nxt}, {"ctx": prv}, other_core, other_group):
+        pl.semaphore_signal(barrier, inc=1, device_id=peer, device_id_type=MESH)
+    pl.semaphore_wait(barrier, 4)
+
+    jobs = job_table(w_ref.shape[0])
+    forward = (True, False, False, True)
+
+    def ring_copy(k, step):
+        size, low, high = jobs[k]
+        rows = pl.ds(pl.multiple_of(low + group * (high - low), SUB), size)
+        if forward[k]:
+            origin, peer = (pos + n - step) % n, nxt
+        else:
+            origin, peer = (pos + step) % n, prv
+        source = w_ref.at[rows] if step == 0 else wbuf.at[origin, rows]
+        return pltpu.make_async_remote_copy(
+            src_ref=source, dst_ref=wbuf.at[origin, rows],
+            send_sem=w_send.at[k, step], recv_sem=w_recv.at[k, step],
+            device_id={"ctx": peer}, device_id_type=MESH,
+        )
+
+    def plane_copy(k, step):
+        size, low, high = jobs[k]
+        rows = pl.ds(pl.multiple_of(low + group * (high - low), SUB), size)
+        origin = (pos + n - 1 - step) % n if forward[k] else (pos + 1 + step) % n
+        return pltpu.make_async_remote_copy(
+            src_ref=wbuf.at[origin, rows], dst_ref=wbuf.at[origin, rows],
+            send_sem=y_send.at[k, step], recv_sem=y_recv.at[k, step],
+            device_id=other_group, device_id_type=MESH,
+        )
+
+    rings = [[ring_copy(k, s) for s in range(n - 1)] for k in range(4)]
+    planes = [[plane_copy(k, s) for s in range(n - 1)] for k in range(2)]
+    for k in range(4):
+        rings[k][0].start()
+
+    def hidden_copies(i):
+        source = hidden_ref.at[:, pl.ds(i * depth, depth)]
+        mine = feats.at[core * in_half + i]
+        swap = pltpu.make_async_remote_copy(
+            src_ref=source, dst_ref=mine, send_sem=hid_sem.at[0, i], recv_sem=hid_sem.at[1, i],
+            device_id=other_core, device_id_type=MESH,
+        )
+        return swap, pltpu.make_async_copy(source, mine, hid_sem.at[2, i])
+
+    for i in range(in_half):
+        for copy in hidden_copies(i):
+            copy.start()
+
+    def consume(origin, chunk, first=False):
+        owner = ring_to_ctx(origin, n)
+        for j in range(per_owner):
+            row = rows_ref[owner * per_owner + j]
+            part = feats[row]
+            term = jnp.dot(
+                part, chunk[j * depth : (j + 1) * depth, :], preferred_element_type=jnp.float32
+            )
+            if first and j == 0:
+                acc[...] = term
+            else:
+                acc[...] += term
+
+    done = {}
+    for distance in range(1, n):
+        done.setdefault(max(distance - 1, n - 1 - distance), []).append(distance)
+
+    for step in range(n - 1):
+        for k in range(4):
+            rings[k][step].wait_recv()
+            if step + 1 < n - 1:
+                rings[k][step + 1].start()
+            if k < 2:
+                planes[k][step].start()
+        if step == 0:
+            for i in range(in_half):
+                for copy in hidden_copies(i):
+                    copy.wait()
+            consume(pos, w_ref, True)
+        if step > 0:
+            for k in range(2):
+                planes[k][step - 1].wait_recv()
+            for distance in done.get(step - 1, ()):
+                origin = (pos + n - distance) % n
+                consume(origin, wbuf.at[origin])
+    for k in range(2):
+        planes[k][n - 2].wait_recv()
+    for distance in done.get(n - 2, ()):
+        origin = (pos + n - distance) % n
+        consume(origin, wbuf.at[origin])
+    for k in range(4):
+        for s in range(n - 1):
+            rings[k][s].wait_send()
+    for k in range(2):
+        for s in range(n - 1):
+            planes[k][s].wait_send()
+
+    kv_ref[ctx] = acc[...].astype(kv_ref.dtype)
+    pieces = kv_ref.shape[1] // kv_rows_piece
+
+    def kv_copy(k, step):
+        rows = pl.ds(k * kv_rows_piece, kv_rows_piece)
+        if k % 2 == 0:
+            origin, peer = ring_to_ctx((pos + n - step) % n, n), nxt
+        else:
+            origin, peer = ring_to_ctx((pos + step) % n, n), prv
+        return pltpu.make_async_remote_copy(
+            src_ref=kv_ref.at[origin, rows], dst_ref=kv_ref.at[origin, rows],
+            send_sem=kv_send.at[k, step], recv_sem=kv_recv.at[k, step],
+            device_id={"ctx": peer}, device_id_type=MESH,
+        )
+
+    moves = [[kv_copy(k, s) for s in range(n - 1)] for k in range(pieces)]
+    for k in range(pieces):
+        moves[k][0].start()
+    for step in range(n - 1):
+        for k in range(pieces):
+            moves[k][step].wait_recv()
+            if step + 1 < n - 1:
+                moves[k][step + 1].start()
+    for k in range(pieces):
+        for s in range(n - 1):
+            moves[k][s].wait_send()
+
+
+def attend_kernel(n, sel_ref, cnt_ref, at_ref, q_ref, kv_ref, out_ref):
+    tok_rows = q_ref.shape[0]
+    block_rows = KB // n
+    start = at_ref[0] * tok_rows
+    q_block = start // KB
+    q = q_ref[...]
+    scale = 1.0 / math.sqrt(HD)
+    offsets = lax.broadcasted_iota(jnp.int32, (KB, 1), 0)
+    within = offsets % block_rows * n + offsets // block_rows
+    q_within = start % KB + lax.broadcasted_iota(jnp.int32, (1, tok_rows), 1)
+
+    def load(block):
+        rows = pl.ds(pl.multiple_of(block * block_rows, block_rows), block_rows)
+        k = kv_ref[:, rows, :HD].reshape(KB, HD)
+        v = kv_ref[:, rows, HD:].reshape(KB, HD)
+        return k, v
+
+    def item(block, masked):
+        k, v = load(block)
+        s = lax.dot_general(k, q, (((1,), (1,)), ((), ())), preferred_element_type=jnp.float32)
+        s = s * scale
+        if masked:
+            s = jnp.where(within <= q_within, s, masked_score)
+        peak = jnp.max(s, axis=0, keepdims=True)
+        raised = jnp.exp(s - peak)
+        total = jnp.sum(raised, axis=0, keepdims=True)
+        blended = lax.dot_general(
+            v, raised.astype(jnp.bfloat16), (((0,), (0,)), ((), ())),
+            preferred_element_type=jnp.float32,
+        )
+        return peak, total, blended
+
+    def more(c, carry):
+        top, total, blended = carry
+        peak_c, total_c, blended_c = item(sel_ref[q_block, c], False)
+        new = jnp.maximum(top, peak_c)
+        old_f = jnp.exp(top - new)
+        new_f = jnp.exp(peak_c - new)
+        return new, total * old_f + total_c * new_f, blended * old_f + blended_c * new_f
+
+    carry = item(q_block, True)
+    top, total, blended = lax.fori_loop(1, cnt_ref[q_block], more, carry)
+    out_ref[...] = (blended / total).T.astype(out_ref.dtype)
+
+
+def ladder_shards(hidden, queries, weight_buckets, bucket_rows, selected, counts):
+    n = lax.axis_size("ctx")
+    tok_rows, half = hidden.shape
+    feat_width = half * lax.axis_size("tp")
+    kv_local = weight_buckets.shape[2]
+    kv_width = kv_local * 2 * HD
+    w = weight_buckets.reshape(-1, kv_width)
+    chunk_rows = w.shape[0]
+    piece = tok_rows // 4
+    vmem = pl.BlockSpec(memory_space=pltpu.VMEM)
+    smem = pl.BlockSpec(memory_space=pltpu.SMEM)
+    dma = pltpu.SemaphoreType.DMA
+    kv = pl.pallas_call(
+        functools.partial(project_kernel, n, piece),
+        out_shape=jax.ShapeDtypeStruct((n, tok_rows, kv_width), jnp.bfloat16),
+        in_specs=[smem, vmem, vmem],
+        out_specs=vmem,
+        scratch_shapes=[
+            pltpu.VMEM((bucket_rows.shape[0], tok_rows, feat_width // bucket_rows.shape[0]), jnp.bfloat16),
+            pltpu.VMEM((n, chunk_rows, kv_width), jnp.bfloat16),
+            pltpu.VMEM((tok_rows, kv_width), jnp.float32),
+            dma((3, bucket_rows.shape[0] // 2)),
+            dma((4, n - 1)), dma((4, n - 1)),
+            dma((2, n - 1)), dma((2, n - 1)),
+            dma((4, n - 1)), dma((4, n - 1)),
+        ],
+        compiler_params=pltpu.CompilerParams(
+            collective_id=0, has_side_effects=True, vmem_limit_bytes=40 * MIB
+        ),
+        name="project",
+    )(bucket_rows, hidden, w)
+
+    heads = queries.shape[1] // HD
+    group = heads // kv_local
+    here = lax.axis_index("ctx").astype(jnp.int32).reshape(1)
+    return pl.pallas_call(
+        functools.partial(attend_kernel, n),
+        out_shape=jax.ShapeDtypeStruct(queries.shape, jnp.bfloat16),
+        grid_spec=pltpu.PrefetchScalarGridSpec(
+            num_scalar_prefetch=3,
+            grid=(heads,),
+            in_specs=[
+                pl.BlockSpec((tok_rows, HD), lambda h, *_: (0, h)),
+                pl.BlockSpec((n, tok_rows, 2 * HD), lambda h, *_: (0, 0, h // group)),
+            ],
+            out_specs=pl.BlockSpec((tok_rows, HD), lambda h, *_: (0, h)),
+        ),
+        compiler_params=pltpu.CompilerParams(vmem_limit_bytes=40 * MIB),
+        name="attend",
+    )(selected, counts, here, queries, kv)
+
+
+def takes_ladder(mesh, hidden, weight_buckets, selected):
+    shape = mesh.shape
+    if shape["groups"] != 2 or shape["tp"] != 2 or shape["ctx"] % 2 or shape["ctx"] > 16:
+        return False
+    tok_rows = hidden.shape[0] // (shape["groups"] * shape["ctx"])
+    block_rows = KB // shape["ctx"]
+    return KB % tok_rows == 0 and block_rows % SUB == 0 and tok_rows % (4 * SUB) == 0
+
+
 def solution(mesh):
     placed = (
         P(("groups", "ctx"), "tp"),
@@ -113,6 +389,11 @@
         P("groups", None),
         P("groups"),
     )
-    return jax.shard_map(
-        shards, mesh=mesh, in_specs=placed, out_specs=P(("groups", "ctx"), "tp"), check_vma=False
-    )
+
+    def run(hidden, queries, weight_buckets, bucket_rows, selected, counts):
+        body = ladder_shards if takes_ladder(mesh, hidden, weight_buckets, selected) else general_shards
+        return jax.shard_map(
+            body, mesh=mesh, in_specs=placed, out_specs=P(("groups", "ctx"), "tp"), check_vma=False
+        )(hidden, queries, weight_buckets, bucket_rows, selected, counts)
+
+    return run

time: 295 us -> 124 us (0.42); the launches traced: 291 us -> 123 us
  waiting for transfers between devices: 149 us -> 0 us
  Pallas kernels: 0 us -> 121 us
  local copies, waits for them, and re-layouts: 70.7 us -> 1.92 us
  matrix products: 23.5 us -> 0 us
  between operations: 13.5 us -> 0.05 us
  starting transfers between devices: 12.7 us -> 0 us
  other arithmetic: 11.1 us -> 0 us
  loops' own time: 10.5 us -> 0 us
    pallas_call x0 -> x2, Pallas kernels: none -> 121 us  [the longest x1 91.7 us: ladder_shards(): pl.pallas_call(functools.partial(project_kernel, n, piece), out_shape=jax...]
    all_gather x2 -> x0, waiting for transfers between devices: 114 us -> none  [the longest x1 108 us: shards(): piece = lax.all_gather(weight_buckets, 'ctx', axis=0, tiled=True)]
    all_to_all x2 -> x0, waiting for transfers between devices: 34.9 us -> none  [the longest x1 34.9 us: shards(): lax.all_to_all(outgoing, 'ctx', split_axis=0, concat_axis=0, tiled=True)]
    dot_general x7 -> x0, matrix products: 23.5 us -> none  [the longest x3 11.5 us: one_item(): jnp.einsum('kgqs,skd->kgqd', raised.astype(jnp.bfloat16), stacked[:, :, 1...]
    unnamed x17 -> x10, local copies, waits for them, and re-layouts: 21.9 us -> 0.3 us
    gather x6 -> x0, local copies, waits for them, and re-layouts: 14.7 us -> none  [the longest x2 11.4 us: shards(): gathered.reshape(tok_rows, bucket_count, bucket_depth)[:, bucket_rows, :]]
    all_gather x1 -> x0, local copies, waits for them, and re-layouts: 14.6 us -> none  [shards(): piece = lax.all_gather(weight_buckets, 'ctx', axis=0, tiled=True)]
    all_to_all x2 -> x0, starting transfers between devices: 12.6 us -> none  [the longest x1 6.62 us: shards(): lax.all_to_all(outgoing, 'ctx', split_axis=0, concat_axis=0, tiled=True)]
  transfers between devices with their start and end apart: 4 -> 0, of which waited for: 3 -> 0; matrix products, arithmetic and copies ran while one was open for 21% -> 0% of each run, Pallas kernels for 0% -> 0%
where the time goes in v1:
time: 124 us; the launch traced here: 123 us
  Pallas kernels  121 us (98%)
  local copies, waits for them, and re-layouts  1.92 us (2%)
    pallas_call x1, Pallas kernels, ladder_shards(): pl.pallas_call(functools.partial(project_kernel, n, piece), out_shape=jax...  91.7 us
    pallas_call x1, Pallas kernels, ladder_shards(): pl.pallas_call(functools.partial(attend_kernel, n), out_shape=jax.ShapeDt...  29.8 us

profile of v1, /device:TPU:24, one launch (start us, length us, event | category | flops | bytes accessed | tf_op | source)
XLA Modules:
  0.0 123.4 jit_solution(7601233937509057226)
XLA Ops:
  0.0 0.0 copy-start.4
  0.0 0.0 copy-start
  0.0 1.6 %reshape.7.w_ref = bf16[1024,512]{1,0:T(8,128)(2,1)S(1)} reshape(bf16[2,512,2,2,128]{4,3,2,1,0:T(2,128)(2,1)} %param.8) | data formatting | bytes 2097152 | tf_op jit(solution)/shard_map/reshape | solution.py:328
  1.6 0.0 copy-done.4
  1.6 0.3 copy-done
  1.9 0.0 copy-start.1
  1.9 0.0 copy-start.2
  1.9 0.0 copy-start.3
  1.9 91.7 %project.1.kv_ref = bf16[8,256,512]{2,1,0:T(8,128)(2,1)S(1)} custom-call(s32[16]{0:T(128)S(1)} %copy-done.4, bf16[256,4096]{1,0:T(8,128)(2,1)S(1)} %copy-done, bf16[1024,512]{1,0:T(8,128)(2,1)S(1)} %reshape.7.w_ref), custom_call_target="tpu_custom_call" | custom-call | tf_op jit(solution)/shard_map/project/pallas_call | solution.py:334
  93.6 0.0 copy-done.1
  93.7 0.0 copy-done.2
  93.7 0.0 copy-done.3
  93.7 29.8 %attend.1 = bf16[256,2048]{1,0:T(8,128)(2,1)} custom-call(s32[4,3]{1,0:T(4,128)S(1)} %copy-done.2, s32[4]{0:T(128)S(1)} %copy-done.3, s32[1]{0:T(128)} %bitcast.at_ref, bf16[256,2048]{1,0:T(8,128)(2,1)S(1)} %copy-done.1, bf16[8,256,512]{2,1,0:T(8,128)(2,1)S(1)} %project.1.kv_ref), custom_call_target="tpu_custom_call" | custom-call | tf_op jit(solution)/shard_map/attend/pallas_call | solution.py:357
Async XLA Ops:
  0.0 1.6 %copy-start.4 = (s32[16]{0:T(128)S(1)}, s32[16]{0:T(128)}, u32[]{:S(2)}) copy-start(s32[16]{0:T(128)} %rows_ref.1) | copy-start | bytes 196
  0.0 1.9 %copy-start = (bf16[256,4096]{1,0:T(8,128)(2,1)S(1)}, bf16[256,4096]{1,0:T(8,128)(2,1)}, u32[]{:S(2)}) copy-start(bf16[256,4096]{1,0:T(8,128)(2,1)} %hidden_ref.1) | copy-start | bytes 6291460
  1.9 91.7 %copy-start.1 = (bf16[256,2048]{1,0:T(8,128)(2,1)S(1)}, bf16[256,2048]{1,0:T(8,128)(2,1)}, u32[]{:S(2)}) copy-start(bf16[256,2048]{1,0:T(8,128)(2,1)} %q_ref.1) | copy-start | bytes 3145732
  1.9 91.7 %copy-start.2 = (s32[4,3]{1,0:T(4,128)S(1)}, s32[4,3]{1,0:T(4,128)}, u32[]{:S(2)}) copy-start(s32[4,3]{1,0:T(4,128)} %sel_ref.1) | copy-start | bytes 148
  1.9 91.7 %copy-start.3 = (s32[4]{0:T(128)S(1)}, s32[4]{0:T(128)}, u32[]{:S(2)}) copy-start(s32[4]{0:T(128)} %cnt_ref.1) | copy-start | bytes 52

commit v2 on v0

--- a/solution.py
+++ b/solution.py
@@ -1,8 +1,11 @@
+import functools
 import math
 
 import jax
 import jax.numpy as jnp
 from jax import lax
+from jax.experimental import pallas as pl
+from jax.experimental.pallas import tpu as pltpu
 from jax.sharding import PartitionSpec as P
 
 HD = 128
@@ -13,7 +16,7 @@
 masked_score = -1e30
 
 
-def shards(hidden, queries, weight_buckets, bucket_rows, selected, counts):
+def general_shards(hidden, queries, weight_buckets, bucket_rows, selected, counts):
     tok_rows = hidden.shape[0]
     ctx_size = lax.axis_size("ctx")
     ctx_index = lax.axis_index("ctx")
@@ -104,6 +107,331 @@
     return result.transpose(0, 3, 1, 2, 4).reshape(tok_rows, heads_local * HD).astype(jnp.bfloat16)
 
 
+SUB = 16
+MESH = pl.DeviceIdType.MESH
+MIB = 1 << 20
+
+
+def ladder_ctx(pos, n):
+    upper = pos // (n // 2)
+    return 2 * pos + upper * (2 * n - 1 - 4 * pos)
+
+
+def ladder_pos(ctx, n):
+    return ctx // 2 + (ctx % 2) * (n - 1 - 2 * (ctx // 2))
+
+
+def project_kernel(
+    n, rows_ref, hidden_ref, w_ref, kv_ref,
+    feats, xfeats, stage, wbuf, acc, psend, precv,
+    hid_sem, w_send, w_recv, x_send, x_recv, f_send, f_recv, p_send, p_recv, kv_send, kv_recv, own_sem,
+):
+    ctx = lax.axis_index("ctx")
+    plane = lax.axis_index("groups")
+    core = lax.axis_index("tp")
+    col = ctx % 2
+    pos = plane * (n - 1) + (ctx // 2) * (1 - 2 * plane)
+    walk = ladder_pos(ctx, n)
+    after = ladder_ctx((walk + 1) % n, n)
+    before = ladder_ctx((walk + n - 1) % n, n)
+    depth = feats.shape[2]
+    width = wbuf.shape[3]
+    in_half = feats.shape[0] // 2
+    share = n // 2
+
+    def node(p):
+        side = p // (n // 2)
+        return side, p * (1 - 2 * side) + side * (n - 1)
+
+    def bucket(p, column):
+        side, level = node(p)
+        return (level * 2 + column) * 2 + side
+
+    def ring_peer(p):
+        side, level = node(p)
+        return {"ctx": level * 2 + col, "groups": side}
+
+    up, down = ring_peer((pos + 1) % n), ring_peer((pos + n - 1) % n)
+    other_core = {"tp": 1 - core}
+    other_col = {"ctx": ctx + 1 - 2 * col}
+
+    barrier = pltpu.get_barrier_semaphore()
+    peers = (up, down, other_core, other_col, {"ctx": after}, {"ctx": before})
+    for peer in peers:
+        pl.semaphore_signal(barrier, inc=1, device_id=peer, device_id_type=MESH)
+    pl.semaphore_wait(barrier, len(peers))
+
+    piece = depth // 4
+
+    def weight_copy(c, k, step):
+        rows = pl.ds(k * piece, piece)
+        if k < 2:
+            origin, peer = (pos + n - step) % n, up
+        else:
+            origin, peer = (pos + step) % n, down
+        if step == 0:
+            source = w_ref.at[plane, rows, pl.ds(c * width, width)]
+        else:
+            source = wbuf.at[c, origin, rows]
+        return pltpu.make_async_remote_copy(
+            src_ref=source, dst_ref=wbuf.at[c, origin, rows],
+            send_sem=w_send.at[c, k, step], recv_sem=w_recv.at[c, k, step],
+            device_id=peer, device_id_type=MESH,
+        )
+
+    def weight_start(c):
+        for k in range(4):
+            weight_copy(c, k, 0).start()
+
+    def weight_step(c, step):
+        for k in range(4):
+            weight_copy(c, k, step).wait_recv()
+            if step + 1 < n - 1:
+                weight_copy(c, k, step + 1).start()
+
+    def own_copy(c):
+        return pltpu.make_async_copy(
+            w_ref.at[plane, :, pl.ds(c * width, width)], wbuf.at[c, pos], own_sem.at[c]
+        )
+
+    def hidden_copies(i):
+        source = hidden_ref.at[:, pl.ds(i * depth, depth)]
+        mine = feats.at[core * in_half + i]
+        swap = pltpu.make_async_remote_copy(
+            src_ref=source, dst_ref=mine, send_sem=hid_sem.at[0, i], recv_sem=hid_sem.at[1, i],
+            device_id=other_core, device_id_type=MESH,
+        )
+        return swap, pltpu.make_async_copy(source, mine, hid_sem.at[2, i])
+
+    def across_copy(i):
+        return pltpu.make_async_remote_copy(
+            src_ref=stage.at[i], dst_ref=xfeats.at[core * share + i],
+            send_sem=x_send.at[i], recv_sem=x_recv.at[i],
+            device_id=other_col, device_id_type=MESH,
+        )
+
+    def pass_copy(i):
+        spot = xfeats.at[core * share + i]
+        return pltpu.make_async_remote_copy(
+            src_ref=spot, dst_ref=spot, send_sem=f_send.at[i], recv_sem=f_recv.at[i],
+            device_id=other_core, device_id_type=MESH,
+        )
+
+    def partial_copy(c):
+        return pltpu.make_async_remote_copy(
+            src_ref=psend.at[c], dst_ref=precv.at[c], send_sem=p_send.at[c], recv_sem=p_recv.at[c],
+            device_id=other_col, device_id_type=MESH,
+        )
+
+    block_rows = KB // n
+
+    def kv_copy(c, k, step):
+        rows = pl.ds(k * block_rows, block_rows)
+        if k % 2 == 0:
+            origin, peer = ladder_ctx((walk + n - step) % n, n), after
+        else:
+            origin, peer = ladder_ctx((walk + step) % n, n), before
+        spot = kv_ref.at[c, origin, rows]
+        return pltpu.make_async_remote_copy(
+            src_ref=spot, dst_ref=spot, send_sem=kv_send.at[c, k, step], recv_sem=kv_recv.at[c, k, step],
+            device_id={"ctx": peer}, device_id_type=MESH,
+        )
+
+    pieces = kv_ref.shape[2] // block_rows
+
+    def partials(c):
+        psend[c] = jnp.zeros(psend.shape[1:], jnp.float32)
+
+        @pl.loop(0, n)
+        def _(p):
+            psend[c] += jnp.dot(xfeats[p], wbuf[c, p], preferred_element_type=jnp.float32)
+
+        partial_copy(c).start()
+        acc[c] = jnp.zeros(acc.shape[1:], jnp.float32)
+
+        @pl.loop(0, n)
+        def _(p):
+            row = rows_ref[bucket(p, col)]
+            acc[c] += jnp.dot(feats[row], wbuf[c, p], preferred_element_type=jnp.float32)
+
+    def kv_start(c):
+        partial_copy(c).wait_recv()
+        kv_ref[c, ctx] = (acc[c] + precv[c]).astype(kv_ref.dtype)
+        for k in range(pieces):
+            kv_copy(c, k, 0).start()
+
+    def kv_step(c, step):
+        for k in range(pieces):
+            kv_copy(c, k, step).wait_recv()
+            if step + 1 < n - 1:
+                kv_copy(c, k, step + 1).start()
+
+    weight_start(0)
+    for i in range(in_half):
+        for copy in hidden_copies(i):
+            copy.start()
+    for c in range(2):
+        own_copy(c).start()
+    steps = n - 1
+    lag = steps - 1
+    for t in range(steps + lag):
+        if t < steps:
+            weight_step(0, t)
+        if t + 1 == lag:
+            weight_start(1)
+        if t >= lag:
+            weight_step(1, t - lag)
+        if t == 1:
+            for i in range(in_half):
+                for copy in hidden_copies(i):
+                    copy.wait()
+            for i in range(share):
+                stage[i] = feats[rows_ref[bucket(core * share + i, 1 - col)]]
+                across_copy(i).start()
+        if t == lag + 3:
+            for i in range(share):
+                across_copy(i).wait_recv()
+                pass_copy(i).start()
+            for c in range(2):
+                own_copy(c).wait()
+        if t == lag + 4:
+            for i in range(share):
+                pass_copy(i).wait_recv()
+            partials(0)
+    partials(1)
+    kv_start(0)
+    kv_lag = 3
+    for t in range(steps + kv_lag):
+        if t < steps:
+            kv_step(0, t)
+        if t + 1 == kv_lag:
+            kv_start(1)
+        if t >= kv_lag:
+            kv_step(1, t - kv_lag)
+
+    for i in range(share):
+        across_copy(i).wait_send()
+        pass_copy(i).wait_send()
+    for c in range(2):
+        partial_copy(c).wait_send()
+        for s in range(steps):
+            for k in range(4):
+                weight_copy(c, k, s).wait_send()
+            for k in range(pieces):
+                kv_copy(c, k, s).wait_send()
+
+
+def attend_kernel(n, sel_ref, cnt_ref, at_ref, q_ref, kv_ref, out_ref):
+    tok_rows = q_ref.shape[0]
+    block_rows = KB // n
+    start = at_ref[0] * tok_rows
+    q_block = start // KB
+    heads = q_ref.shape[1] // HD
+    scale = math.log2(math.e) / math.sqrt(HD)
+    offsets = lax.broadcasted_iota(jnp.int32, (1, KB), 1)
+    within = offsets % block_rows * n + offsets // block_rows
+    q_within = start % KB + lax.broadcasted_iota(jnp.int32, (tok_rows, 1), 0)
+
+    def item(block, head, masked):
+        rows = pl.ds(pl.multiple_of(block * block_rows, block_rows), block_rows)
+        k = kv_ref[0, :, rows, :HD].reshape(KB, HD)
+        v = kv_ref[0, :, rows, HD:].reshape(KB, HD)
+        q = q_ref[:, head * HD : (head + 1) * HD]
+        s = lax.dot_general(q, k, (((1,), (1,)), ((), ())), preferred_element_type=jnp.float32)
+        if masked:
+            s = jnp.where(within <= q_within, s, masked_score)
+        peak = jnp.max(s, axis=1, keepdims=True)
+        raised = jnp.exp2((s - peak) * scale)
+        total = jnp.sum(raised, axis=1, keepdims=True)
+        blended = jnp.dot(raised.astype(jnp.bfloat16), v, preferred_element_type=jnp.float32)
+        return peak, total, blended
+
+    def more(c, carry):
+        merged = []
+        for head, (top, total, blended) in enumerate(carry):
+            peak_c, total_c, blended_c = item(sel_ref[q_block, c], head, False)
+            new = jnp.maximum(top, peak_c)
+            old_f = jnp.exp2((top - new) * scale)
+            new_f = jnp.exp2((peak_c - new) * scale)
+            merged.append((new, total * old_f + total_c * new_f, blended * old_f + blended_c * new_f))
+        return tuple(merged)
+
+    carry = tuple(item(q_block, head, True) for head in range(heads))
+    carry = lax.fori_loop(1, cnt_ref[q_block], more, carry)
+    for head, (_, total, blended) in enumerate(carry):
+        out_ref[:, head * HD : (head + 1) * HD] = (blended / total).astype(out_ref.dtype)
+
+
+def ladder_shards(hidden, queries, weight_buckets, bucket_rows, selected, counts):
+    n = lax.axis_size("ctx")
+    tok_rows, half = hidden.shape
+    buckets = bucket_rows.shape[0]
+    depth = half * lax.axis_size("tp") // buckets
+    owned, _, kv_local = weight_buckets.shape[:3]
+    width = 2 * HD
+    w = weight_buckets.reshape(owned, depth, kv_local * width)
+    vmem = pl.BlockSpec(memory_space=pltpu.VMEM)
+    smem = pl.BlockSpec(memory_space=pltpu.SMEM)
+    dma = pltpu.SemaphoreType.DMA
+    pieces = tok_rows * n // KB
+    f32 = jnp.float32
+    bf16 = jnp.bfloat16
+    kv = pl.pallas_call(
+        functools.partial(project_kernel, n),
+        out_shape=jax.ShapeDtypeStruct((kv_local, n, tok_rows, width), bf16),
+        in_specs=[smem, vmem, vmem],
+        out_specs=vmem,
+        scratch_shapes=[
+            pltpu.VMEM((buckets, tok_rows, depth), bf16),
+            pltpu.VMEM((n, tok_rows, depth), bf16),
+            pltpu.VMEM((n // 2, tok_rows, depth), bf16),
+            pltpu.VMEM((kv_local, n, depth, width), bf16),
+            pltpu.VMEM((kv_local, tok_rows, width), f32),
+            pltpu.VMEM((kv_local, tok_rows, width), f32),
+            pltpu.VMEM((kv_local, tok_rows, width), f32),
+            dma((3, buckets // 2)),
+            dma((kv_local, 4, n - 1)), dma((kv_local, 4, n - 1)),
+            dma((n // 2,)), dma((n // 2,)), dma((n // 2,)), dma((n // 2,)),
+            dma((kv_local,)), dma((kv_local,)),
+            dma((kv_local, pieces, n - 1)), dma((kv_local, pieces, n - 1)),
+            dma((kv_local,)),
+        ],
+        compiler_params=pltpu.CompilerParams(
+            collective_id=0, has_side_effects=True, vmem_limit_bytes=40 * MIB
+        ),
+        name="project",
+    )(bucket_rows, hidden, w)
+
+    group = queries.shape[1] // kv_local
+    here = lax.axis_index("ctx").astype(jnp.int32).reshape(1)
+    return pl.pallas_call(
+        functools.partial(attend_kernel, n),
+        out_shape=jax.ShapeDtypeStruct(queries.shape, bf16),
+        grid_spec=pltpu.PrefetchScalarGridSpec(
+            num_scalar_prefetch=3,
+            grid=(kv_local,),
+            in_specs=[
+                pl.BlockSpec((tok_rows, group), lambda h, *_: (0, h)),
+                pl.BlockSpec((1, n, tok_rows, width), lambda h, *_: (h, 0, 0, 0)),
+            ],
+            out_specs=pl.BlockSpec((tok_rows, group), lambda h, *_: (0, h)),
+        ),
+        compiler_params=pltpu.CompilerParams(vmem_limit_bytes=40 * MIB),
+        name="attend",
+    )(selected, counts, here, queries, kv)
+
+
+def takes_ladder(mesh, hidden, weight_buckets):
+    shape = mesh.shape
+    n = shape["ctx"]
+    if shape["groups"] != 2 or shape["tp"] != 2 or n % 2 or n > 16:
+        return False
+    tok_rows = hidden.shape[0] // (2 * n)
+    buckets, depth, heads = weight_buckets.shape[:3]
+    fits = buckets == 2 * n and depth % (4 * SUB) == 0 and heads == 4
+    return fits and KB % tok_rows == 0 and KB // n % SUB == 0
+
+
 def solution(mesh):
     placed = (
         P(("groups", "ctx"), "tp"),
@@ -113,6 +441,11 @@
         P("groups", None),
         P("groups"),
     )
-    return jax.shard_map(
-        shards, mesh=mesh, in_specs=placed, out_specs=P(("groups", "ctx"), "tp"), check_vma=False
-    )
+
+    def run(hidden, queries, weight_buckets, bucket_rows, selected, counts):
+        body = ladder_shards if takes_ladder(mesh, hidden, weight_buckets) else general_shards
+        return jax.shard_map(
+            body, mesh=mesh, in_specs=placed, out_specs=P(("groups", "ctx"), "tp"), check_vma=False
+        )(hidden, queries, weight_buckets, bucket_rows, selected, counts)
+
+    return run

time: 295 us -> 121 us (0.41); the launches traced: 291 us -> 121 us
  waiting for transfers between devices: 149 us -> 0 us
  Pallas kernels: 0 us -> 119 us
  local copies, waits for them, and re-layouts: 70.7 us -> 1.92 us
  matrix products: 23.5 us -> 0 us
  between operations: 13.5 us -> 0.05 us
  starting transfers between devices: 12.7 us -> 0 us
  other arithmetic: 11.1 us -> 0 us
  loops' own time: 10.5 us -> 0 us
    pallas_call x0 -> x2, Pallas kernels: none -> 119 us  [the longest x1 98.5 us: ladder_shards(): pl.pallas_call(functools.partial(project_kernel, n), out_shape=jax.ShapeD...]
    all_gather x2 -> x0, waiting for transfers between devices: 114 us -> none  [the longest x1 108 us: shards(): piece = lax.all_gather(weight_buckets, 'ctx', axis=0, tiled=True)]
    all_to_all x2 -> x0, waiting for transfers between devices: 34.9 us -> none  [the longest x1 34.9 us: shards(): lax.all_to_all(outgoing, 'ctx', split_axis=0, concat_axis=0, tiled=True)]
    dot_general x7 -> x0, matrix products: 23.5 us -> none  [the longest x3 11.5 us: one_item(): jnp.einsum('kgqs,skd->kgqd', raised.astype(jnp.bfloat16), stacked[:, :, 1...]
    unnamed x17 -> x10, local copies, waits for them, and re-layouts: 21.9 us -> 0.3 us
    gather x6 -> x0, local copies, waits for them, and re-layouts: 14.7 us -> none  [the longest x2 11.4 us: shards(): gathered.reshape(tok_rows, bucket_count, bucket_depth)[:, bucket_rows, :]]
    all_gather x1 -> x0, local copies, waits for them, and re-layouts: 14.6 us -> none  [shards(): piece = lax.all_gather(weight_buckets, 'ctx', axis=0, tiled=True)]
    all_to_all x2 -> x0, starting transfers between devices: 12.6 us -> none  [the longest x1 6.62 us: shards(): lax.all_to_all(outgoing, 'ctx', split_axis=0, concat_axis=0, tiled=True)]
  transfers between devices with their start and end apart: 4 -> 0, of which waited for: 3 -> 0; matrix products, arithmetic and copies ran while one was open for 21% -> 0% of each run, Pallas kernels for 0% -> 0%
where the time goes in v2:
time: 121 us
  Pallas kernels  119 us (98%)
  local copies, waits for them, and re-layouts  1.92 us (2%)
    pallas_call x1, Pallas kernels, ladder_shards(): pl.pallas_call(functools.partial(project_kernel, n), out_shape=jax.ShapeD...  98.5 us
    pallas_call x1, Pallas kernels, ladder_shards(): pl.pallas_call(functools.partial(attend_kernel, n), out_shape=jax.ShapeDt...  20.6 us

profile of v2, /device:TPU:24, one launch (start us, length us, event | category | flops | bytes accessed | tf_op | source)
XLA Modules:
  0.0 121.0 jit_solution(4965458239267709958)
XLA Ops:
  0.0 0.0 copy-start.4
  0.0 0.0 copy-start
  0.0 1.6 %reshape.7.w_ref = bf16[2,512,512]{2,1,0:T(8,128)(2,1)S(1)} reshape(bf16[2,512,2,2,128]{4,3,2,1,0:T(2,128)(2,1)} %param.8) | data formatting | bytes 2097152 | tf_op jit(solution)/shard_map/reshape | solution.py:372
  1.6 0.0 copy-done.4
  1.6 0.3 copy-done
  1.9 0.0 copy-start.1
  1.9 0.0 copy-start.2
  1.9 0.0 copy-start.3
  1.9 98.5 %project.1.kv_ref = bf16[2,8,256,256]{3,2,1,0:T(8,128)(2,1)S(1)} custom-call(s32[16]{0:T(128)S(1)} %copy-done.4, bf16[256,4096]{1,0:T(8,128)(2,1)S(1)} %copy-done, bf16[2,512,512]{2,1,0:T(8,128)(2,1)S(1)} %reshape.7.w_ref), custom_call_target="tpu_custom_call" | custom-call | tf_op jit(solution)/shard_map/project/pallas_call | solution.py:379
  100.4 0.0 copy-done.1
  100.4 0.0 copy-done.2
  100.4 0.0 copy-done.3
  100.5 20.6 %attend.1 = bf16[256,2048]{1,0:T(8,128)(2,1)} custom-call(s32[4,3]{1,0:T(4,128)S(1)} %copy-done.2, s32[4]{0:T(128)S(1)} %copy-done.3, s32[1]{0:T(128)} %bitcast.at_ref, bf16[256,2048]{1,0:T(8,128)(2,1)S(1)} %copy-done.1, bf16[2,8,256,256]{3,2,1,0:T(8,128)(2,1)S(1)} %project.1.kv_ref), custom_call_target="tpu_custom_call" | custom-call | tf_op jit(solution)/shard_map/attend/pallas_call | solution.py:407
Async XLA Ops:
  0.0 1.6 %copy-start.4 = (s32[16]{0:T(128)S(1)}, s32[16]{0:T(128)}, u32[]{:S(2)}) copy-start(s32[16]{0:T(128)} %rows_ref.1) | copy-start | bytes 196
  0.0 1.9 %copy-start = (bf16[256,4096]{1,0:T(8,128)(2,1)S(1)}, bf16[256,4096]{1,0:T(8,128)(2,1)}, u32[]{:S(2)}) copy-start(bf16[256,4096]{1,0:T(8,128)(2,1)} %hidden_ref.1) | copy-start | bytes 6291460
  1.9 98.5 %copy-start.1 = (bf16[256,2048]{1,0:T(8,128)(2,1)S(1)}, bf16[256,2048]{1,0:T(8,128)(2,1)}, u32[]{:S(2)}) copy-start(bf16[256,2048]{1,0:T(8,128)(2,1)} %q_ref.1) | copy-start | bytes 3145732
  1.9 98.5 %copy-start.2 = (s32[4,3]{1,0:T(4,128)S(1)}, s32[4,3]{1,0:T(4,128)}, u32[]{:S(2)}) copy-start(s32[4,3]{1,0:T(4,128)} %sel_ref.1) | copy-start | bytes 148
  1.9 98.5 %copy-start.3 = (s32[4]{0:T(128)S(1)}, s32[4]{0:T(128)}, u32[]{:S(2)}) copy-start(s32[4]{0:T(128)} %cnt_ref.1) | copy-start | bytes 52

commit v3 on v2

--- a/solution.py
+++ b/solution.py
@@ -179,20 +179,38 @@
             device_id=peer, device_id_type=MESH,
         )
 
+    def weight_goes(k, step):
+        return (2 * pos + (2 + n - step if k < 2 else step)) % n != 0
+
+    def weight_comes(k, step):
+        return (2 * pos + (n - step if k < 2 else 2 + step)) % n != 0
+
+    def weight_send(c, k, step):
+        @pl.when(weight_goes(k, step))
+        def _():
+            weight_copy(c, k, step).start()
+
     def weight_start(c):
         for k in range(4):
-            weight_copy(c, k, 0).start()
+            weight_send(c, k, 0)
 
     def weight_step(c, step):
         for k in range(4):
-            weight_copy(c, k, step).wait_recv()
+            @pl.when(weight_comes(k, step))
+            def _():
+                weight_copy(c, k, step).wait_recv()
+
             if step + 1 < n - 1:
-                weight_copy(c, k, step + 1).start()
-
-    def own_copy(c):
-        return pltpu.make_async_copy(
-            w_ref.at[plane, :, pl.ds(c * width, width)], wbuf.at[c, pos], own_sem.at[c]
-        )
+                weight_send(c, k, step + 1)
+
+    def own_copies(c):
+        columns = pl.ds(c * width, width)
+        return [
+            pltpu.make_async_copy(
+                w_ref.at[side, :, columns], wbuf.at[c, spot], own_sem.at[c, i]
+            )
+            for i, (side, spot) in enumerate(((plane, pos), (1 - plane, n - 1 - pos)))
+        ]
 
     def hidden_copies(i):
         source = hidden_ref.at[:, pl.ds(i * depth, depth)]
@@ -266,14 +284,18 @@
             if step + 1 < n - 1:
                 kv_copy(c, k, step + 1).start()
 
+    for c in range(2):
+        for copy in own_copies(c):
+            copy.start()
     weight_start(0)
     for i in range(in_half):
         for copy in hidden_copies(i):
             copy.start()
     for c in range(2):
-        own_copy(c).start()
+        for copy in own_copies(c):
+            copy.wait()
     steps = n - 1
-    lag = steps - 1
+    lag = 1
     for t in range(steps + lag):
         if t < steps:
             weight_step(0, t)
@@ -288,26 +310,20 @@
             for i in range(share):
                 stage[i] = feats[rows_ref[bucket(core * share + i, 1 - col)]]
                 across_copy(i).start()
-        if t == lag + 3:
+        if t == steps + lag - 2:
             for i in range(share):
                 across_copy(i).wait_recv()
                 pass_copy(i).start()
-            for c in range(2):
-                own_copy(c).wait()
-        if t == lag + 4:
+        if t == steps + lag - 1:
             for i in range(share):
                 pass_copy(i).wait_recv()
             partials(0)
     partials(1)
-    kv_start(0)
-    kv_lag = 3
-    for t in range(steps + kv_lag):
-        if t < steps:
-            kv_step(0, t)
-        if t + 1 == kv_lag:
-            kv_start(1)
-        if t >= kv_lag:
-            kv_step(1, t - kv_lag)
+    for c in range(2):
+        kv_start(c)
+    for t in range(steps):
+        for c in range(2):
+            kv_step(c, t)
 
     for i in range(share):
         across_copy(i).wait_send()
@@ -316,7 +332,10 @@
         partial_copy(c).wait_send()
         for s in range(steps):
             for k in range(4):
-                weight_copy(c, k, s).wait_send()
+                @pl.when(weight_goes(k, s))
+                def _():
+                    weight_copy(c, k, s).wait_send()
+
             for k in range(pieces):
                 kv_copy(c, k, s).wait_send()
 
@@ -394,7 +413,7 @@
             dma((n // 2,)), dma((n // 2,)), dma((n // 2,)), dma((n // 2,)),
             dma((kv_local,)), dma((kv_local,)),
             dma((kv_local, pieces, n - 1)), dma((kv_local, pieces, n - 1)),
-            dma((kv_local,)),
+            dma((kv_local, 2)),
         ],
         compiler_params=pltpu.CompilerParams(
             collective_id=0, has_side_effects=True, vmem_limit_bytes=40 * MIB

time: 121 us -> 107 us (0.88)
  Pallas kernels: 119 us -> 105 us
    pallas_call x1, Pallas kernels: 98.5 us -> 83.9 us  [ladder_shards(): pl.pallas_call(functools.partial(project_kernel, n), out_shape=jax.ShapeD...]
where the time goes in v3:
time: 107 us; the launch traced here: 106 us
  Pallas kernels  105 us (98%)
  local copies, waits for them, and re-layouts  1.92 us (2%)
    pallas_call x1, Pallas kernels, ladder_shards(): pl.pallas_call(functools.partial(project_kernel, n), out_shape=jax.ShapeD...  83.9 us
    pallas_call x1, Pallas kernels, ladder_shards(): pl.pallas_call(functools.partial(attend_kernel, n), out_shape=jax.ShapeDt...  20.6 us

profile of v3, /device:TPU:24, one launch (start us, length us, event | category | flops | bytes accessed | tf_op | source)
XLA Modules:
  0.0 106.5 jit_solution(5246084655342961255)
XLA Ops:
  0.0 0.0 copy-start.4
  0.0 0.0 copy-start
  0.0 1.6 %reshape.7.w_ref = bf16[2,512,512]{2,1,0:T(8,128)(2,1)S(1)} reshape(bf16[2,512,2,2,128]{4,3,2,1,0:T(2,128)(2,1)} %param.8) | data formatting | bytes 2097152 | tf_op jit(solution)/shard_map/reshape | solution.py:391
  1.6 0.0 copy-done.4
  1.6 0.3 copy-done
  1.9 0.0 copy-start.1
  1.9 0.0 copy-start.2
  1.9 0.0 copy-start.3
  1.9 83.9 %project.1.kv_ref = bf16[2,8,256,256]{3,2,1,0:T(8,128)(2,1)S(1)} custom-call(s32[16]{0:T(128)S(1)} %copy-done.4, bf16[256,4096]{1,0:T(8,128)(2,1)S(1)} %copy-done, bf16[2,512,512]{2,1,0:T(8,128)(2,1)S(1)} %reshape.7.w_ref), custom_call_target="tpu_custom_call" | custom-call | tf_op jit(solution)/shard_map/project/pallas_call | solution.py:398
  85.9 0.0 copy-done.1
  85.9 0.0 copy-done.2
  85.9 0.0 copy-done.3
  85.9 20.6 %attend.1 = bf16[256,2048]{1,0:T(8,128)(2,1)} custom-call(s32[4,3]{1,0:T(4,128)S(1)} %copy-done.2, s32[4]{0:T(128)S(1)} %copy-done.3, s32[1]{0:T(128)} %bitcast.at_ref, bf16[256,2048]{1,0:T(8,128)(2,1)S(1)} %copy-done.1, bf16[2,8,256,256]{3,2,1,0:T(8,128)(2,1)S(1)} %project.1.kv_ref), custom_call_target="tpu_custom_call" | custom-call | tf_op jit(solution)/shard_map/attend/pallas_call | solution.py:426
Async XLA Ops:
  0.0 1.6 %copy-start.4 = (s32[16]{0:T(128)S(1)}, s32[16]{0:T(128)}, u32[]{:S(2)}) copy-start(s32[16]{0:T(128)} %rows_ref.1) | copy-start | bytes 196
  0.0 1.9 %copy-start = (bf16[256,4096]{1,0:T(8,128)(2,1)S(1)}, bf16[256,4096]{1,0:T(8,128)(2,1)}, u32[]{:S(2)}) copy-start(bf16[256,4096]{1,0:T(8,128)(2,1)} %hidden_ref.1) | copy-start | bytes 6291460
  1.9 84.0 %copy-start.1 = (bf16[256,2048]{1,0:T(8,128)(2,1)S(1)}, bf16[256,2048]{1,0:T(8,128)(2,1)}, u32[]{:S(2)}) copy-start(bf16[256,2048]{1,0:T(8,128)(2,1)} %q_ref.1) | copy-start | bytes 3145732
  1.9 84.0 %copy-start.2 = (s32[4,3]{1,0:T(4,128)S(1)}, s32[4,3]{1,0:T(4,128)}, u32[]{:S(2)}) copy-start(s32[4,3]{1,0:T(4,128)} %sel_ref.1) | copy-start | bytes 148
  1.9 84.0 %copy-start.3 = (s32[4]{0:T(128)S(1)}, s32[4]{0:T(128)}, u32[]{:S(2)}) copy-start(s32[4]{0:T(128)} %cnt_ref.1) | copy-start | bytes 52

commit v4 on v3

--- a/solution.py
+++ b/solution.py
@@ -265,6 +265,8 @@
             psend[c] += jnp.dot(xfeats[p], wbuf[c, p], preferred_element_type=jnp.float32)
 
         partial_copy(c).start()
+
+    def own_sums(c):
         acc[c] = jnp.zeros(acc.shape[1:], jnp.float32)
 
         @pl.loop(0, n)
@@ -319,6 +321,8 @@
                 pass_copy(i).wait_recv()
             partials(0)
     partials(1)
+    for c in range(2):
+        own_sums(c)
     for c in range(2):
         kv_start(c)
     for t in range(steps):

time: 107 us -> 107 us (level)
  no operation moved by 1% of the time
where the time goes in v4:
time: 107 us; the launch traced here: 106 us
  Pallas kernels  105 us (98%)
  local copies, waits for them, and re-layouts  1.92 us (2%)
    pallas_call x1, Pallas kernels, ladder_shards(): pl.pallas_call(functools.partial(project_kernel, n), out_shape=jax.ShapeD...  83.9 us
    pallas_call x1, Pallas kernels, ladder_shards(): pl.pallas_call(functools.partial(attend_kernel, n), out_shape=jax.ShapeDt...  20.6 us

profile of v4, /device:TPU:24, one launch (start us, length us, event | category | flops | bytes accessed | tf_op | source)
XLA Modules:
  0.0 106.5 jit_solution(11873844923258278419)
XLA Ops:
  0.0 0.0 copy-start.4
  0.0 0.0 copy-start
  0.0 1.6 %reshape.7.w_ref = bf16[2,512,512]{2,1,0:T(8,128)(2,1)S(1)} reshape(bf16[2,512,2,2,128]{4,3,2,1,0:T(2,128)(2,1)} %param.8) | data formatting | bytes 2097152 | tf_op jit(solution)/shard_map/reshape | solution.py:395
  1.6 0.0 copy-done.4
  1.6 0.3 copy-done
  1.9 0.0 copy-start.1
  1.9 0.0 copy-start.2
  1.9 0.0 copy-start.3
  1.9 83.9 %project.1.kv_ref = bf16[2,8,256,256]{3,2,1,0:T(8,128)(2,1)S(1)} custom-call(s32[16]{0:T(128)S(1)} %copy-done.4, bf16[256,4096]{1,0:T(8,128)(2,1)S(1)} %copy-done, bf16[2,512,512]{2,1,0:T(8,128)(2,1)S(1)} %reshape.7.w_ref), custom_call_target="tpu_custom_call" | custom-call | tf_op jit(solution)/shard_map/project/pallas_call | solution.py:402
  85.9 0.0 copy-done.1
  85.9 0.0 copy-done.2
  85.9 0.0 copy-done.3
  85.9 20.6 %attend.1 = bf16[256,2048]{1,0:T(8,128)(2,1)} custom-call(s32[4,3]{1,0:T(4,128)S(1)} %copy-done.2, s32[4]{0:T(128)S(1)} %copy-done.3, s32[1]{0:T(128)} %bitcast.at_ref, bf16[256,2048]{1,0:T(8,128)(2,1)S(1)} %copy-done.1, bf16[2,8,256,256]{3,2,1,0:T(8,128)(2,1)S(1)} %project.1.kv_ref), custom_call_target="tpu_custom_call" | custom-call | tf_op jit(solution)/shard_map/attend/pallas_call | solution.py:430
Async XLA Ops:
  0.0 1.6 %copy-start.4 = (s32[16]{0:T(128)S(1)}, s32[16]{0:T(128)}, u32[]{:S(2)}) copy-start(s32[16]{0:T(128)} %rows_ref.1) | copy-start | bytes 196
  0.0 1.9 %copy-start = (bf16[256,4096]{1,0:T(8,128)(2,1)S(1)}, bf16[256,4096]{1,0:T(8,128)(2,1)}, u32[]{:S(2)}) copy-start(bf16[256,4096]{1,0:T(8,128)(2,1)} %hidden_ref.1) | copy-start | bytes 6291460
  1.9 84.0 %copy-start.1 = (bf16[256,2048]{1,0:T(8,128)(2,1)S(1)}, bf16[256,2048]{1,0:T(8,128)(2,1)}, u32[]{:S(2)}) copy-start(bf16[256,2048]{1,0:T(8,128)(2,1)} %q_ref.1) | copy-start | bytes 3145732
  1.9 84.0 %copy-start.2 = (s32[4,3]{1,0:T(4,128)S(1)}, s32[4,3]{1,0:T(4,128)}, u32[]{:S(2)}) copy-start(s32[4,3]{1,0:T(4,128)} %sel_ref.1) | copy-start | bytes 148
  1.9 84.0 %copy-start.3 = (s32[4]{0:T(128)S(1)}, s32[4]{0:T(128)}, u32[]{:S(2)}) copy-start(s32[4]{0:T(128)} %cnt_ref.1) | copy-start | bytes 52
